TPU v7x, 768 devices: a whole 4x8x12 slice. The times are simulated.
768 devices in a mesh: row: 16 (over y, z_hi), col: 12 (over z_lo, core), chan: 4 (over x).
Axes of the slice: x: 4, y: 8, z: 12 (z_hi: 2, z_lo: 6; z = z_hi * 6 + z_lo), core: 2. Of those that a mesh axis runs over, the one named last changes fastest.
Arguments:
- velocity: float32 [16, 3, 256, 3072], P('chan', None, 'row', 'col'), may hold values from -6 to 6
- lift_weight: float32 [32, 3], replicated, may hold values from -3.5 to 3.5
- lift_bias: float32 [32], replicated, may hold values from -3 to 3
- conv_weight: bfloat16 [27, 32, 32], P(None, 'chan'), may hold values from -0.21875 to 0.21875
- conv_bias: bfloat16 [32], P('chan'), may hold values from -3 to 3
- head_weight: bfloat16 [6, 32], P(None, 'chan'), may hold values from -1 to 1
Outputs:
- velocity_next: float32 [16, 3, 256, 3072], P('chan', None, 'row', 'col')
- stress: float32 [8, 6, 128, 1536], P('chan', None, 'row', 'col')
All inputs are finite; a program needn't handle non-finite values.
Results may differ from a plain program's by a relative error of at most 0.0003.
Values may be sent and summed in bfloat16 or wider, within the bound.
A program may use at most 64 MiB of HBM per device.

v0:
```python
import jax
import jax.numpy as jnp
from jax import lax
from jax.sharding import PartitionSpec as P

step_size = 0.1


def padded_2(cells, sides, width):
    for axis, dim in sides:
        count = lax.axis_size(axis)
        head = lax.slice_in_dim(cells, 0, width, axis=dim)
        tail = lax.slice_in_dim(cells, cells.shape[dim] - width, cells.shape[dim], axis=dim)
        cells = jnp.concatenate(
            [
                lax.ppermute(tail, axis, [(i, (i + 1) % count) for i in range(count)]),
                cells,
                lax.ppermute(head, axis, [((i + 1) % count, i) for i in range(count)]),
            ],
            axis=dim,
        )
    return cells


def coarsen(velocity):
    nplanes, comps, ylen, zlen = velocity.shape
    blocks = velocity.reshape(nplanes // 2, 2, comps, ylen // 2, 2, zlen // 2, 2)
    return jnp.mean(blocks, axis=(1, 4, 6))


def lift(box, lift_weight, lift_bias):
    linear = jnp.einsum("ci,xiyz->xcyz", lift_weight, box, precision=lax.Precision.HIGHEST)
    return jnp.tanh(linear + lift_bias[None, :, None, None])


def upsample(field):
    return jnp.repeat(jnp.repeat(jnp.repeat(field, 2, 0), 2, 2), 2, 3)


def fluxes(velocity, fine):
    ux = velocity[:, 0]
    uy = velocity[:, 1]
    uz = velocity[:, 2]
    return jnp.stack(
        [
            ux * ux + fine[:, 0],
            uy * uy + fine[:, 1],
            uz * uz + fine[:, 2],
            ux * uy + fine[:, 3],
            ux * uz + fine[:, 4],
            uy * uz + fine[:, 5],
        ],
        axis=1,
    )


def closure_rows(hidden, weights, biases, header, count):
    ylen = hidden.shape[2] - 2
    zlen = hidden.shape[3] - 2
    wide_weights = weights.astype(jnp.float32)
    total = jnp.zeros((count, weights.shape[1], ylen, zlen), jnp.float32)
    for shift_x in range(3):
        for shift_y in range(3):
            for shift_z in range(3):
                offset = 9 * shift_x + 3 * shift_y + shift_z
                piece = hidden[
                    shift_x : shift_x + count, :, shift_y : shift_y + ylen, shift_z : shift_z + zlen
                ]
                total = total + jnp.einsum(
                    "oi,xiyz->xoyz", wide_weights[offset], piece, precision=lax.Precision.HIGHEST
                )
    activation = jax.nn.silu(total + biases.astype(jnp.float32)[None, :, None, None])
    return jnp.einsum(
        "so,xoyz->xsyz", header.astype(jnp.float32), activation, precision=lax.Precision.HIGHEST
    )


def derive(padded, axis):
    length = padded.shape[axis] - 6

    def moved(offset):
        selector = [slice(3, -3), slice(None), slice(3, -3), slice(3, -3)]
        selector[axis] = slice(offset, offset + length)
        return padded[tuple(selector)]

    return (
        45.0 * (moved(4) - moved(2)) - 9.0 * (moved(5) - moved(1)) + (moved(6) - moved(0))
    ) / 60.0


def body(velocity, lift_weight, lift_bias, conv_weight, conv_bias, head_weight):
    box = coarsen(velocity)
    planes = box.shape[0]
    gathered = lax.all_gather(box, "chan", axis=0, tiled=True)
    rimmed = padded_2(gathered, (("row", 2), ("col", 3)), 1)
    hidden = lift(rimmed, lift_weight, lift_bias)
    hidden = jnp.concatenate([hidden[-1:], hidden, hidden[:1]], 0)
    stress = lax.psum_scatter(
        closure_rows(hidden, conv_weight, conv_bias, head_weight, lax.axis_size("chan") * planes),
        "chan",
        scatter_dimension=0,
        tiled=True,
    )
    flux = fluxes(velocity, upsample(stress))
    padded = padded_2(flux, (("row", 2), ("col", 3), ("chan", 0)), 3)
    along_x = derive(padded, 0)
    along_y = derive(padded, 2)
    along_z = derive(padded, 3)
    first = along_x[:, 0] + along_y[:, 3] + along_z[:, 4]
    second = along_x[:, 3] + along_y[:, 1] + along_z[:, 5]
    third = along_x[:, 4] + along_y[:, 5] + along_z[:, 2]
    divergence = jnp.stack([first, second, third], axis=1)
    return (velocity - step_size * divergence, stress)


def solution(mesh):
    placed = (
        P("chan", None, "row", "col"),
        P(),
        P(),
        P(None, "chan", None),
        P("chan"),
        P(None, "chan"),
    )
    return jax.shard_map(
        body,
        mesh=mesh,
        in_specs=placed,
        out_specs=(P("chan", None, "row", "col"), P("chan", None, "row", "col")),
        check_vma=False,
    )
```

profile of v0, /device:TPU:1, one launch (start us, length us, event | category | flops | bytes accessed | tf_op | source)
XLA Modules:
  0.0 202.1 jit_solution(18167358432377760989)
XLA Ops:
  7.2 14.7 %reshape.18 = f32[2,2,3,8,2,128,2]{6,5,4,3,2,1,0:T(8,128)} reshape(f32[4,3,16,256]{3,2,1,0:T(8,128)} %param.6) | data formatting | bytes 393216 | tf_op jit(solution)/shard_map/reshape | solution.py:27
  21.9 5.5 %reduce_sum.9 = f32[2,3,8,128]{3,2,1,0:T(8,128)S(1)} reduce(f32[2,2,3,8,2,128,2]{6,5,4,3,2,1,0:T(8,128)} %reshape.18, f32[]{:T(128)} %constant.5.clone.1), dimensions={1,4,6}, to_apply=%region_0.0 | reduce | flops 43008 | bytes 221188 | tf_op jit(solution)/shard_map/reduce_sum | solution.py:28
  27.4 10.2 %all_gather.3 = f32[8,3,8,128]{3,2,1,0:T(8,128)S(1)} all-gather(f32[2,3,8,128]{3,2,1,0:T(8,128)S(1)} %broadcast_multiply_fusion), channel_id=1, replica_groups=mesh['row'=16,'col'=12,'chan'=4] {'chan'}, dimensions={0}, use_global_device_ids=true | all-gather | bytes 122880 | tf_op jit(solution)/shard_map/all_gather | solution.py:94
  37.7 14.9 %collective-permute-start = (f32[8,3,1,128]{3,1,2,0:T(4,128)S(1)}, f32[8,3,1,128]{3,1,2,0:T(4,128)S(1)}, u32[]{:S(2)}, u32[]{:S(2)}) collective-permute-start(f32[8,3,1,128]{3,1,2,0:T(4,128)S(1)} %copy.186), channel_id=1, source_target_pairs={{0,48},{48,96},{96,144},{144,192},{192,240},{240,288},{288,336},{3... | collective-permute-start | bytes 36872 | tf_op jit(solution)/shard_map/ppermute | solution.py:16
  52.6 4.8 %collective-permute-start.1 = (f32[8,3,1,128]{3,1,2,0:T(4,128)S(1)}, f32[8,3,1,128]{3,1,2,0:T(4,128)S(1)}, u32[]{:S(2)}, u32[]{:S(2)}) collective-permute-start(f32[8,3,1,128]{3,1,2,0:T(4,128)S(1)} %copy.187), channel_id=1, source_target_pairs={{48,0},{96,48},{144,96},{192,144},{240,192},{288,240},{336,288},{3... | collective-permute-start | bytes 36872 | tf_op jit(solution)/shard_map/ppermute | solution.py:18
  57.5 6.1 %collective-permute-done.1 = f32[8,3,1,128]{3,1,2,0:T(4,128)S(1)} collective-permute-done((f32[8,3,1,128]{3,1,2,0:T(4,128)S(1)}, f32[8,3,1,128]{3,1,2,0:T(4,128)S(1)}, u32[]{:S(2)}, u32[]{:S(2)}) %collective-permute-start.1) | collective-permute-done | bytes 12320 | tf_op jit(solution)/shard_map/ppermute | solution.py:18
  63.7 7.8 %collective-permute-start.2 = (f32[8,3,10,1]{3,1,2,0:T(4,128)S(1)}, f32[8,3,10,1]{3,1,2,0:T(4,128)S(1)}, u32[]{:S(2)}, u32[]{:S(2)}) collective-permute-start(f32[8,3,10,1]{3,1,2,0:T(4,128)S(1)} %get-tuple-element.42), channel_id=1, source_target_pairs={{0,4},{4,8},{8,12},{12,16},{16,20},{20,24},{24,28},{28,32},{32,36}... | collective-permute-start | bytes 2888 | tf_op jit(solution)/shard_map/ppermute | solution.py:16
  71.5 2.1 %collective-permute-start.3 = (f32[8,3,10,1]{3,1,2,0:T(4,128)S(1)}, f32[8,3,10,1]{3,1,2,0:T(4,128)S(1)}, u32[]{:S(2)}, u32[]{:S(2)}) collective-permute-start(f32[8,3,10,1]{3,1,2,0:T(4,128)S(1)} %get-tuple-element.43), channel_id=1, source_target_pairs={{4,0},{8,4},{12,8},{16,12},{20,16},{24,20},{28,24},{32,28},{36,32}... | collective-permute-start | bytes 2888 | tf_op jit(solution)/shard_map/ppermute | solution.py:18
  73.8 6.2 %collective-permute-done.3 = f32[8,3,10,1]{3,1,2,0:T(4,128)S(1)} collective-permute-done((f32[8,3,10,1]{3,1,2,0:T(4,128)S(1)}, f32[8,3,10,1]{3,1,2,0:T(4,128)S(1)}, u32[]{:S(2)}, u32[]{:S(2)}) %collective-permute-start.3) | collective-permute-done | bytes 992 | tf_op jit(solution)/shard_map/ppermute | solution.py:18
  79.9 2.3 %tanh_bitcast_fusion = f32[8,32,10,130]{3,1,2,0:T(8,128)S(1)} fusion(f32[32]{0:T(128)S(1)} %copy-done.4, f32[8,3,10,1]{3,1,2,0:T(4,128)S(1)} %collective-permute-done.3, f32[8,3,10,128]{3,1,2,0:T(4,128)S(1)} %constant_dynamic-update-slice_fusion, f32[8,3,10,1]{3,1,2,0:T(4,128)S(1)} %collective-permute-done.2, f32[32,3]{0,1:T(4,128)S(1)} %copy-done), kind=kOutput, calls=%fused_computation.32 | convolution fusion | flops 12376000 | bytes 1456512 | tf_op jit(solution)/shard_map/ci,xiyz->xcyz/dot_general | solution.py:32
  82.8 0.6 convolution_bitcast_fusion.8
  83.4 0.6 convolution_bitcast_fusion.7
  84.5 0.6 convolution_bitcast_fusion.5
  85.1 0.6 convolution_bitcast_fusion.4
  86.2 0.6 convolution_bitcast_fusion.2
  86.8 0.6 convolution_bitcast_fusion.1
  88.5 0.6 convolution_add_fusion.15
  89.1 0.6 convolution_add_fusion.14
  90.2 0.6 convolution_add_fusion.12
  90.8 0.6 convolution_add_fusion.11
  91.9 0.8 convolution_add_fusion.9
  92.7 0.6 convolution_add_fusion.8
  93.8 0.6 convolution_add_fusion.6
  94.4 0.6 convolution_add_fusion.5
  96.1 0.6 convolution_add_fusion.2
  97.2 0.7 fusion.11
  97.8 1.0 convolution_bitcast_fusion
  98.9 27.1 %reduce-scatter.2.cloned.1.call-done = f32[2,6,8,128]{3,1,2,0:T(8,128)} async-done(((f32[8,6,8,128]{3,1,2,0:T(8,128)}), f32[2,6,8,128]{3,1,2,0:T(8,128)}) %reduce-scatter.2.cloned.1.call-update) | async-done | bytes 49168 | tf_op jit(solution)/shard_map/reduce_scatter | solution.py:98
  126.0 0.8 copy.97
  127.4 1.1 broadcast_in_dim.13
  128.6 1.1 fusion.170
  129.6 1.2 copy.150
  131.9 10.1 %collective-permute-start.4 = (f32[4,6,3,256]{3,0,2,1:T(4,128)S(1)}, f32[4,6,3,256]{3,0,2,1:T(4,128)S(1)}, u32[]{:S(2)}, u32[]{:S(2)}) collective-permute-start(f32[4,6,3,256]{3,0,2,1:T(4,128)S(1)} %copy.105), channel_id=1, source_target_pairs={{0,48},{48,96},{96,144},{144,192},{192,240},{240,288},{288,336},{3... | collective-permute-start | bytes 221192 | tf_op jit(solution)/shard_map/ppermute | solution.py:16
  142.1 4.2 %collective-permute-start.5 = (f32[4,6,3,256]{3,0,2,1:T(4,128)S(1)}, f32[4,6,3,256]{3,0,2,1:T(4,128)S(1)}, u32[]{:S(2)}, u32[]{:S(2)}) collective-permute-start(f32[4,6,3,256]{3,0,2,1:T(4,128)S(1)} %copy.106), channel_id=1, source_target_pairs={{48,0},{96,48},{144,96},{192,144},{240,192},{288,240},{336,288},{3... | collective-permute-start | bytes 221192 | tf_op jit(solution)/shard_map/ppermute | solution.py:18
  146.6 7.3 %collective-permute-done.5 = f32[4,6,3,256]{3,0,2,1:T(4,128)S(1)} collective-permute-done((f32[4,6,3,256]{3,0,2,1:T(4,128)S(1)}, f32[4,6,3,256]{3,0,2,1:T(4,128)S(1)}, u32[]{:S(2)}, u32[]{:S(2)}) %collective-permute-start.5) | collective-permute-done | bytes 73760 | tf_op jit(solution)/shard_map/ppermute | solution.py:18
  154.2 7.5 %collective-permute-start.6 = (f32[4,6,22,3]{3,0,2,1:T(4,128)S(1)}, f32[4,6,22,3]{3,0,2,1:T(4,128)S(1)}, u32[]{:S(2)}, u32[]{:S(2)}) collective-permute-start(f32[4,6,22,3]{3,0,2,1:T(4,128)S(1)} %get-tuple-element.39), channel_id=1, source_target_pairs={{0,4},{4,8},{8,12},{12,16},{16,20},{20,24},{24,28},{28,32},{32,36}... | collective-permute-start | bytes 19016 | tf_op jit(solution)/shard_map/ppermute | solution.py:16
  161.7 1.9 collective-permute-start.7
  163.7 1.4 collective-permute-done.6
  165.1 7.6 %collective-permute-done.7 = f32[4,6,22,3]{3,0,2,1:T(4,128)S(1)} collective-permute-done((f32[4,6,22,3]{3,0,2,1:T(4,128)S(1)}, f32[4,6,22,3]{3,0,2,1:T(4,128)S(1)}, u32[]{:S(2)}, u32[]{:S(2)}) %collective-permute-start.7) | collective-permute-done | bytes 6368 | tf_op jit(solution)/shard_map/ppermute | solution.py:18
  172.6 0.6 pad_maximum_fusion.4
  173.6 1.9 collective-permute-start.9
  175.6 4.8 %collective-permute-start.8 = (f32[3,6,22,262]{3,2,1,0:T(8,128)S(1)}, f32[3,6,22,262]{3,2,1,0:T(8,128)S(1)}, u32[]{:S(2)}, u32[]{:S(2)}) collective-permute-start(f32[3,6,22,262]{3,2,1,0:T(8,128)S(1)} %copy.189), channel_id=1, source_target_pairs={{1,0},{2,1},{3,2},{0,3},{5,4},{6,5},{7,6},{4,7},{9,8},{10,9},{11,1... | collective-permute-start | bytes 1245032 | tf_op jit(solution)/shard_map/ppermute | solution.py:18
  180.5 1.8 fusion.70
  182.3 0.6 fusion.61
  182.9 9.9 %collective-permute-done.9 = f32[3,6,22,262]{3,2,1,0:T(8,128)S(1)} collective-permute-done((f32[3,6,22,262]{3,2,1,0:T(8,128)S(1)}, f32[3,6,22,262]{3,2,1,0:T(8,128)S(1)}, u32[]{:S(2)}, u32[]{:S(2)}) %collective-permute-start.9) | collective-permute-done | bytes 415040 | tf_op jit(solution)/shard_map/ppermute | solution.py:16
  193.0 0.8 collective-permute-done.8
  193.8 0.7 fusion.73
  194.6 0.7 fusion.92
  (70 shorter events, 8.7 us)
Async XLA Ops:
  7.2 72.7 %copy-start = (f32[32,3]{0,1:T(4,128)S(1)}, f32[32,3]{0,1:T(4,128)}, u32[]{:S(2)}) copy-start(f32[32,3]{0,1:T(4,128)} %param.7) | copy-start | bytes 1156
  7.2 118.8 %reduce-scatter.2.cloned.1.call-start = ((), (), s32[]{:S(2)}) async-start(), calls=%async_computation.1 | async-start | bytes 327680 | tf_op jit(solution)/shard_map/reduce_scatter | solution.py:98
  21.9 51.7 %copy-start.6 = (bf16[8]{0:T(256)(128)(2,1)S(1)}, bf16[8]{0:T(256)(128)(2,1)}, u32[]{:S(2)}) copy-start(bf16[8]{0:T(256)(128)(2,1)} %param.10) | copy-start | bytes 52
  21.9 58.0 %copy-start.4 = (f32[32]{0:T(128)S(1)}, f32[32]{0:T(128)}, u32[]{:S(2)}) copy-start(f32[32]{0:T(128)} %param.8) | copy-start | bytes 388
  37.7 19.7 %collective-permute-start = (f32[8,3,1,128]{3,1,2,0:T(4,128)S(1)}, f32[8,3,1,128]{3,1,2,0:T(4,128)S(1)}, u32[]{:S(2)}, u32[]{:S(2)}) collective-permute-start(f32[8,3,1,128]{3,1,2,0:T(4,128)S(1)} %copy.186), channel_id=1, source_target_pairs={{0,48},{48,96},{96,144},{144,192},{192,240},{240,288},{288,336},{3... | collective-permute-start | bytes 36872 | tf_op jit(solution)/shard_map/ppermute | solution.py:16
  52.6 11.0 %collective-permute-start.1 = (f32[8,3,1,128]{3,1,2,0:T(4,128)S(1)}, f32[8,3,1,128]{3,1,2,0:T(4,128)S(1)}, u32[]{:S(2)}, u32[]{:S(2)}) collective-permute-start(f32[8,3,1,128]{3,1,2,0:T(4,128)S(1)} %copy.187), channel_id=1, source_target_pairs={{48,0},{96,48},{144,96},{192,144},{240,192},{288,240},{336,288},{3... | collective-permute-start | bytes 36872 | tf_op jit(solution)/shard_map/ppermute | solution.py:18
  57.4 24.9 %copy-start.3 = (bf16[27,8,32]{2,1,0:T(8,128)(2,1)S(1)}, bf16[27,8,32]{2,1,0:T(8,128)(2,1)}, u32[]{:S(2)}) copy-start(bf16[27,8,32]{2,1,0:T(8,128)(2,1)} %param.9) | copy-start | bytes 41476
  63.7 10.0 %collective-permute-start.2 = (f32[8,3,10,1]{3,1,2,0:T(4,128)S(1)}, f32[8,3,10,1]{3,1,2,0:T(4,128)S(1)}, u32[]{:S(2)}, u32[]{:S(2)}) collective-permute-start(f32[8,3,10,1]{3,1,2,0:T(4,128)S(1)} %get-tuple-element.42), channel_id=1, source_target_pairs={{0,4},{4,8},{8,12},{12,16},{16,20},{20,24},{24,28},{28,32},{32,36}... | collective-permute-start | bytes 2888 | tf_op jit(solution)/shard_map/ppermute | solution.py:16
  71.5 8.4 %collective-permute-start.3 = (f32[8,3,10,1]{3,1,2,0:T(4,128)S(1)}, f32[8,3,10,1]{3,1,2,0:T(4,128)S(1)}, u32[]{:S(2)}, u32[]{:S(2)}) collective-permute-start(f32[8,3,10,1]{3,1,2,0:T(4,128)S(1)} %get-tuple-element.43), channel_id=1, source_target_pairs={{4,0},{8,4},{12,8},{16,12},{20,16},{24,20},{28,24},{32,28},{36,32}... | collective-permute-start | bytes 2888 | tf_op jit(solution)/shard_map/ppermute | solution.py:18
  96.7 1.2 copy-start.5
  126.8 1.7 copy-start.2
  128.5 2.3 %copy-start.1 = (f32[4,3,16,256]{3,2,1,0:T(8,128)S(1)}, f32[4,3,16,256]{3,2,1,0:T(8,128)}, u32[]{:S(2)}) copy-start(f32[4,3,16,256]{3,2,1,0:T(8,128)} %param.6) | copy-start | bytes 589828
  131.9 14.4 %collective-permute-start.4 = (f32[4,6,3,256]{3,0,2,1:T(4,128)S(1)}, f32[4,6,3,256]{3,0,2,1:T(4,128)S(1)}, u32[]{:S(2)}, u32[]{:S(2)}) collective-permute-start(f32[4,6,3,256]{3,0,2,1:T(4,128)S(1)} %copy.105), channel_id=1, source_target_pairs={{0,48},{48,96},{96,144},{144,192},{192,240},{240,288},{288,336},{3... | collective-permute-start | bytes 221192 | tf_op jit(solution)/shard_map/ppermute | solution.py:16
  142.1 11.9 %collective-permute-start.5 = (f32[4,6,3,256]{3,0,2,1:T(4,128)S(1)}, f32[4,6,3,256]{3,0,2,1:T(4,128)S(1)}, u32[]{:S(2)}, u32[]{:S(2)}) collective-permute-start(f32[4,6,3,256]{3,0,2,1:T(4,128)S(1)} %copy.106), channel_id=1, source_target_pairs={{48,0},{96,48},{144,96},{192,144},{240,192},{288,240},{336,288},{3... | collective-permute-start | bytes 221192 | tf_op jit(solution)/shard_map/ppermute | solution.py:18
  154.2 10.9 %collective-permute-start.6 = (f32[4,6,22,3]{3,0,2,1:T(4,128)S(1)}, f32[4,6,22,3]{3,0,2,1:T(4,128)S(1)}, u32[]{:S(2)}, u32[]{:S(2)}) collective-permute-start(f32[4,6,22,3]{3,0,2,1:T(4,128)S(1)} %get-tuple-element.39), channel_id=1, source_target_pairs={{0,4},{4,8},{8,12},{12,16},{16,20},{20,24},{24,28},{28,32},{32,36}... | collective-permute-start | bytes 19016 | tf_op jit(solution)/shard_map/ppermute | solution.py:16
  161.7 10.9 %collective-permute-start.7 = (f32[4,6,22,3]{3,0,2,1:T(4,128)S(1)}, f32[4,6,22,3]{3,0,2,1:T(4,128)S(1)}, u32[]{:S(2)}, u32[]{:S(2)}) collective-permute-start(f32[4,6,22,3]{3,0,2,1:T(4,128)S(1)} %get-tuple-element.38), channel_id=1, source_target_pairs={{4,0},{8,4},{12,8},{16,12},{20,16},{24,20},{28,24},{32,28},{36,32}... | collective-permute-start | bytes 19016 | tf_op jit(solution)/shard_map/ppermute | solution.py:18
  173.6 19.2 %collective-permute-start.9 = (f32[3,6,22,262]{3,2,1,0:T(8,128)S(1)}, f32[3,6,22,262]{3,2,1,0:T(8,128)S(1)}, u32[]{:S(2)}, u32[]{:S(2)}) collective-permute-start(f32[3,6,22,262]{3,2,1,0:T(8,128)S(1)} %copy.188), channel_id=1, source_target_pairs={{0,1},{1,2},{2,3},{3,0},{4,5},{5,6},{6,7},{7,4},{8,9},{9,10},{10,1... | collective-permute-start | bytes 1245032 | tf_op jit(solution)/shard_map/ppermute | solution.py:16
  175.6 18.1 %collective-permute-start.8 = (f32[3,6,22,262]{3,2,1,0:T(8,128)S(1)}, f32[3,6,22,262]{3,2,1,0:T(8,128)S(1)}, u32[]{:S(2)}, u32[]{:S(2)}) collective-permute-start(f32[3,6,22,262]{3,2,1,0:T(8,128)S(1)} %copy.189), channel_id=1, source_target_pairs={{1,0},{2,1},{3,2},{0,3},{5,4},{6,5},{7,6},{4,7},{9,8},{10,9},{11,1... | collective-permute-start | bytes 1245032 | tf_op jit(solution)/shard_map/ppermute | solution.py:18
Sparse Core Ops, SparseCore 0:
  99.0 26.9 reduce-scatter.1
where the time goes:
time: 204 us; the launch traced here: 202 us
  waiting for transfers between devices  66.4 us (33%)
  starting transfers between devices  60.1 us (29%)
  local copies, waits for them, and re-layouts  22 us (11%)
  matrix products  18.6 us (9%)
  between operations  14.7 us (7%)
  blocking collectives  10.2 us (5%)
  other arithmetic  10.1 us (5%)
    ppermute x5, starting transfers between devices, padded_2(): lax.ppermute(tail, axis, [(i, (i + 1) % count) for i in range(count)])  42.2 us
    ppermute x5, waiting for transfers between devices, padded_2(): lax.ppermute(head, axis, [((i + 1) % count, i) for i in range(count)])  27.9 us
    reduce_scatter x1, waiting for transfers between devices, body(): lax.psum_scatter(closure_rows(hidden, conv_weight, conv_bias, head_weight...  27.1 us
    ppermute x5, starting transfers between devices, padded_2(): lax.ppermute(head, axis, [((i + 1) % count, i) for i in range(count)])  17.9 us
    dot_general x27, matrix products, closure_rows(): jnp.einsum('oi,xiyz->xoyz', wide_weights[offset], piece, precision=lax.Pr...  15.3 us
    reshape x1, local copies, waits for them, and re-layouts, coarsen(): velocity.reshape(nplanes // 2, 2, comps, ylen // 2, 2, zlen // 2, 2)  14.7 us
    ppermute x5, waiting for transfers between devices, padded_2(): lax.ppermute(tail, axis, [(i, (i + 1) % count) for i in range(count)])  11.4 us
    all_gather x1, blocking collectives, body(): gathered = lax.all_gather(box, 'chan', axis=0, tiled=True)  10.2 us
  transfers between devices with their start and end apart: 11, of which 9 were waited for; matrix products, arithmetic and copies ran while one was open for 2% of the time, Pallas kernels for 0%

commit v1 on v0

v1 whole, which is shorter than its diff:
```python
import jax
import jax.numpy as jnp
from jax import lax
from jax.experimental import pallas as pl
from jax.experimental.pallas import tpu as pltpu
from jax.sharding import PartitionSpec as P

MESH = pl.DeviceIdType.MESH
F32 = jnp.float32
BF16 = jnp.bfloat16
NROW, NCOL, NCHAN = 16, 12, 4
ZROWS = 144
COEFS = ((1, 45.0), (2, -9.0), (3, 1.0))
X_COMPS = (0, 3, 4)
Y_COMPS = (3, 1, 5)
Z_COMPS = (4, 5, 2)

PEERS = [
    (dr, dc, dx)
    for dr in (-1, 0, 1)
    for dc in (-1, 0, 1)
    for dx in (-1, 0, 1)
    if (dr, dc, dx) != (0, 0, 0)
] + [(0, 0, 2)]


def iota(shape, dim):
    return lax.broadcasted_iota(jnp.int32, shape, dim)


def split(value):
    high = value.astype(BF16)
    return high, (value - high.astype(F32)).astype(BF16)


def split3(value):
    high = value.astype(BF16)
    rest = value - high.astype(F32)
    mid = rest.astype(BF16)
    return high, mid, (rest - mid.astype(F32)).astype(BF16)


def mm(a, b, dims=((1,), (0,)), exact=False):
    return lax.dot_general(
        a,
        b,
        (dims, ((), ())),
        preferred_element_type=F32,
        precision=lax.Precision.HIGHEST if exact else None,
    )


NT = ((1,), (1,))
TN = ((0,), (0,))


def mm2(value, matrix):
    high, low = split(value)
    rows = value.shape[0]
    both = mm(jnp.concatenate([high, low], 0), matrix)
    return both[:rows] + both[rows:]


def stencil_matrix(distance):
    total = jnp.zeros(distance.shape, F32)
    for k, c in COEFS:
        total = jnp.where(distance == k, c, jnp.where(distance == -k, -c, total))
    return total.astype(BF16)


def body_kernel(
    vel_in, lift_w_in, lift_b_in, conv_w_in, conv_b_in, head_w_in,
    out, stress_out,
    vel, lift_w, lift_b, conv_w, conv_b, head_w,
    xs, bx, ysend, csend, zvsend, yvsend, yvstage, wall,
    yland, cland, xland, zvland, yvland, xv, stx, sland,
    hid, taps, headk, strs, field, edge, base, e2, zd,
    send_sem, recv_sem, load_sem,
):
    here = (lax.axis_index("row"), lax.axis_index("col"), lax.axis_index("chan"))
    me = here[2]

    def peer(off):
        return tuple(
            h if o == 0 else lax.rem(h + (o + n) % n, n)
            for h, o, n in zip(here, off, (NROW, NCOL, NCHAN))
        )

    barrier = pltpu.get_barrier_semaphore()
    for off in PEERS:
        pl.semaphore_signal(barrier, inc=1, device_id=peer(off), device_id_type=MESH)

    pairs_in = (
        (vel_in, vel), (conv_w_in, conv_w), (lift_w_in, lift_w), (lift_b_in, lift_b),
        (conv_b_in, conv_b), (head_w_in, head_w),
    )
    loads = [
        pltpu.make_async_copy(src, dst, load_sem.at[k]) for k, (src, dst) in enumerate(pairs_in)
    ]
    for load in loads:
        load.start()
    copies = []

    def send(src, dst, source, landed=None):
        k = len(copies)
        copy = pltpu.make_async_remote_copy(
            src_ref=src, dst_ref=dst, send_sem=send_sem.at[k], recv_sem=recv_sem.at[k],
            device_id=peer(tuple(-s for s in source)), device_id_type=MESH,
        )
        copy.start()
        if landed is not None:
            copies.append((copy, pltpu.make_async_remote_copy(
                src_ref=src, dst_ref=landed, send_sem=send_sem.at[k], recv_sem=recv_sem.at[k],
                device_id=peer(tuple(-s for s in source)), device_id_type=MESH,
            )))
        else:
            copies.append((copy, copy))
        return k

    def arrive(ks):
        for k in ks:
            copies[k][1].wait_recv()

    pool = jnp.where(iota((256, 128), 0) // 2 == iota((256, 128), 1), 1.0, 0.0).astype(BF16)
    r16 = iota((16, 256), 0)
    ends = jnp.where(r16 < 4, r16, r16 + 120)
    picker = jnp.where((iota((16, 256), 1) // 2 == ends) & (r16 < 8), 1.0, 0.0).astype(BF16)
    csend[...] = jnp.zeros_like(csend)
    loads[0].wait()
    for p in range(2):
        for c in range(3):
            both = vel[2 * p, c] + vel[2 * p + 1, c]
            r = 16 * (3 * p + c)
            xs[0, r : r + 16, :] = both[:, :128]
            xs[1, r : r + 16, :] = both[:, 128:]
    pairs = jnp.concatenate(
        [xs[h, pl.ds(0, 48, 2), :] + xs[h, pl.ds(1, 48, 2), :] for h in range(2)], axis=1
    )
    pieces = split3(pairs * 0.125)
    pooled = mm(jnp.concatenate(pieces, 0), pool)
    box = pooled[0:48] + pooled[48:96] + pooled[96:144]
    bx[0] = box[0:24]
    bx[1] = box[24:48]
    for p in range(2):
        for c in range(3):
            r = 8 * (3 * p + c)
            ysend[0, p, c] = box[r + 4 : r + 8]
            ysend[1, p, c] = box[r : r + 4]
    columns = mm(picker, pieces[0], NT) + mm(picker, pieces[1], NT) + mm(picker, pieces[2], NT)
    csend[0, :, 0:48] = columns[4:8]
    csend[1, :, 0:48] = columns[0:4]
    for k in range(12):
        yvstage[0, 4 * k : 4 * k + 4, :] = vel[k // 3, k % 3, 12:16, :]
        yvstage[1, 4 * k : 4 * k + 4, :] = vel[k // 3, k % 3, 0:4, :]
    slot = iota((48, 256), 0) % 4
    for s, near, spare in ((0, 3, 0), (1, 0, 3)):
        high, low = split(yvstage[s])
        moved = pltpu.roll(low.astype(F32), (spare - near) % 48, 0)
        yvsend[s] = jnp.where(slot == spare, moved, high.astype(F32)).astype(BF16)

    pl.semaphore_wait(barrier, len(PEERS))

    ybox, corner, ycols, yvel = [], [], [], []
    for s, dr in ((0, -1), (1, 1)):
        ybox.append(send(ysend.at[s], yland.at[s, 1:3], (dr, 0, 0)))
    for s, dr in ((0, -1), (1, 1)):
        ybox.append(send(ysend.at[s, 1], yland.at[s, 0], (dr, 0, -1)))
        ybox.append(send(ysend.at[s, 0], yland.at[s, 3], (dr, 0, 1)))
    for s, dr in ((1, -1), (2, 1)):
        for t, dc in ((0, -1), (1, 1)):
            for dx in (-1, 0, 1):
                corner.append(send(csend.at[t], cland.at[s, t, dx + 1], (dr, dc, dx)))
    for t, dc in ((0, -1), (1, 1)):
        for dx in (-1, 0, 1):
            ycols.append(send(csend.at[t], cland.at[0, t, dx + 1], (0, dc, dx)))
    xbox = [send(bx.at[1], xland.at[0], (0, 0, -1)), send(bx.at[0], xland.at[1], (0, 0, 1))]
    for s, dr in ((0, -1), (1, 1)):
        yvel.append(send(yvsend.at[s], yvland.at[s], (dr, 0, 0)))

    for load in loads[1:]:
        load.wait()
    for k in range(9):
        a, c = k // 3, k % 3
        parts = [conv_w[9 * a + 3 * b + c].astype(F32) for b in range(3)]
        wall[me, 8 * k : 8 * k + 8, :] = jnp.concatenate(parts + [jnp.zeros((8, 32), F32)], axis=1)
    wall[me, 72:80, :] = jnp.zeros((8, 128), F32)
    wall[me, 72:78, 0:8] = head_w[...].astype(F32)
    wall[me, 78:79, 0:8] = conv_b[...].astype(F32)
    weights = [
        send(wall.at[me], wall.at[me], (0, 0, dx), wall.at[lax.rem(me + (dx + 4) % 4, 4)])
        for dx in (-1, 1, 2)
    ]
    rz = iota((16, 256), 0)
    at = jnp.where(rz < 8, rz + 248, rz - 8)
    take = jnp.where(iota((16, 256), 1) == at, 1.0, 0.0)
    zvsend[...] = jnp.zeros_like(zvsend)
    for c in range(3):
        cols = mm(take, vel[:, c].reshape(64, 256), NT, exact=True)
        zvsend[0, c, :, 0:64] = cols[0:8]
        zvsend[1, c, :, 0:64] = cols[8:16]
    zvel = [send(zvsend.at[t], zvland.at[t], (0, dc, 0)) for t, dc in ((0, -1), (1, 1))]
    xvel = [send(vel.at[1:4], xv.at[0], (0, 0, -1)), send(vel.at[0:3], xv.at[1], (0, 0, 1))]

    spread = jnp.where(iota((32, 256), 1) % 32 == iota((32, 256), 0), 1.0, 0.0)
    bias = mm(lift_b[...], spread, exact=True)
    rows24 = jnp.where(iota((24, 3), 0) // 8 == iota((24, 3), 1), 1.0, 0.0)
    lift = mm(rows24, mm(lift_w[...], spread, exact=True), exact=True)
    lift = jnp.where(iota((24, 256), 0) % 8 == iota((24, 256), 1) // 32, lift, 0.0)
    lift_of = [
        jnp.concatenate([lift, jnp.zeros((104, 256), F32)], 0),
        jnp.concatenate([jnp.zeros((24, 256), F32), lift, jnp.zeros((80, 256), F32)], 0),
    ]

    def hold(q, row, lane, value):
        high, low = split(value)
        n, m = value.shape
        hid[q, row : row + n, lane : lane + m] = high
        hid[q, ZROWS + row : ZROWS + row + n, lane : lane + m] = low

    def lifted(rows):
        return jnp.tanh(mm(rows, lift, TN, exact=True) + bias)

    def side(s, dx):
        return jnp.concatenate(
            [cland[s, 1, dx + 1], jnp.zeros((8, 128), F32), cland[s, 0, dx + 1]], 0
        )

    PLANES = ((0, -1, 1), (1, 0, 0), (2, 0, 1), (3, 1, 0))
    for p in range(2):
        hold(p + 1, 0, 128, lifted(bx[p]))
    arrive(xbox)
    hold(0, 0, 128, lifted(xland[0]))
    hold(3, 0, 128, lifted(xland[1]))

    arrive(weights)
    lane = iota((32, 128), 1)
    zero = jnp.zeros((32, 128), F32)
    for k in range(9):
        a, c = k // 3, k % 3
        x = jnp.concatenate([wall[n, 8 * k : 8 * k + 8, :] for n in range(4)], 0)
        r1, r2, r3 = (pltpu.roll(x, 32 * n, 1) for n in (1, 2, 3))
        tiles = (
            (r1, zero),
            (jnp.where(lane >= 64, r2, 0.0), jnp.where(lane < 64, r2, 0.0)),
            (jnp.where(lane >= 96, r3, 0.0), jnp.where(lane < 96, r3, 0.0)),
            (zero, x),
        )
        for y, (first, second) in enumerate(tiles):
            r = 128 * c + 32 * y
            taps[a, r : r + 32, 0:128] = first.astype(BF16)
            taps[a, r : r + 32, 128:256] = second.astype(BF16)
    params = wall[0, 72:80, :]
    for n in range(1, 4):
        params = params + pltpu.roll(wall[n, 72:80, :], 8 * n, 1)
    rolled = [params] + [pltpu.roll(params, 32 * n, 1) for n in (1, 2, 3)]
    conv_bias = (rolled[0] + rolled[1] + rolled[2] + rolled[3])[6:7]
    for n in range(4):
        headk[pl.ds(n, 8, 4), :] = rolled[n]
    head = headk[...].astype(BF16)

    arrive(ycols)
    for q, dx, p in PLANES:
        hold(q, 128, 128, jnp.tanh(mm(side(0, dx), lift_of[p], exact=True) + bias))

    def closure(g):
        total = None
        for a in range(3):
            block = hid[a : a + 2, :, 128 * g : 128 * g + 256].reshape(4 * ZROWS, 256)
            term = mm(block, taps[a], NT)
            total = term if total is None else total + term
        for p in range(2):
            r = 2 * ZROWS * p
            both = total[r : r + ZROWS] + total[r + ZROWS : r + 2 * ZROWS]
            conv = (
                pltpu.roll(both[:, 0:128], 1, 0)
                + both[:, 128:256]
                + pltpu.roll(both[:, 256:384], ZROWS - 1, 0)
                + conv_bias
            )
            act = 0.5 * conv * (1.0 + jnp.tanh(0.5 * conv))
            high, low = split(act)
            found = mm(head, high, NT) + mm(head, low, NT)
            for s in range(6):
                strs[p, s, 4 * g : 4 * g + 4, 0:ZROWS] = found[4 * s : 4 * s + 4]

    closure(1)

    field[...] = jnp.zeros_like(field)
    for p in range(4):
        uy = vel[p, 1]
        for i in range(3):
            field[p, i, 8:24, :] = uy * vel[p, i]
    stencil = stencil_matrix(iota((256, 256), 0) - iota((256, 256), 1))
    for i in range(3):
        flux = (vel[:, 2] * vel[:, i]).reshape(64, 256)
        base[:, i] = mm2(flux, stencil).reshape(4, 16, 256)
    for p in range(4):
        for i in range(3):
            total = base[p, i]
            for k, c in COEFS:
                total = total + c * (field[p, i, 8 + k : 24 + k, :] - field[p, i, 8 - k : 24 - k, :])
            base[p, i] = total
    arrive(zvel)
    r16z = iota((16, 256), 0)
    place = jnp.where(r16z < 8, r16z - 8, r16z + 248)
    rim = stencil_matrix(place - iota((16, 256), 1)).astype(F32)
    cols = [jnp.concatenate([zvland[0, c], zvland[1, c]], 0)[:, 0:64] for c in range(3)]
    for i in range(3):
        base[:, i] += mm(cols[2] * cols[i], rim, TN, exact=True).reshape(4, 16, 256)
    arrive(xvel)
    for i in range(3):
        planes = (
            [xv[0, n, 0] * xv[0, n, i] for n in range(3)]
            + [vel[n, 0] * vel[n, i] for n in range(4)]
            + [xv[1, n, 0] * xv[1, n, i] for n in range(3)]
        )
        for p in range(4):
            total = base[p, i]
            for k, c in COEFS:
                total = total + c * (planes[p + 3 + k] - planes[p + 3 - k])
            base[p, i] = total

    arrive(ybox)
    for q in range(4):
        rows = jnp.concatenate(
            [jnp.concatenate([yland[1, q, c], yland[0, q, c]], 0) for c in range(3)], 0
        )
        h = lifted(rows)
        hold(q, 0, 0, h[:, 128:256])
        hold(q, 0, 384, h[:, 0:128])
    arrive(corner)
    for q, dx, p in PLANES:
        rows = jnp.concatenate([side(1, dx), side(2, dx)], 0)
        h = jnp.tanh(mm(rows, lift_of[p], exact=True) + bias)
        hold(q, 128, 0, h[0:16, 128:256])
        hold(q, 128, 384, h[16:32, 0:128])
    closure(0)
    closure(2)

    for p in range(2):
        for i, s in enumerate(X_COMPS):
            stx[p, i] = strs[p, s, 2:10, 0:128]
    xstress = [send(stx, sland.at[0], (0, 0, -1)), send(stx, sland.at[1], (0, 0, 1))]

    for p in range(2):
        for s in range(6):
            stress_out[p, s] = strs[p, s, 2:10, 0:128]

    arrive(yvel)
    edge[...] = jnp.zeros_like(edge)
    both_sides = []
    for s, near, spare in ((0, 3, 0), (1, 0, 3)):
        rows = yvland[s].astype(F32)
        low = pltpu.roll(rows, (near - spare) % 48, 0)
        both_sides.append(rows + jnp.where(slot == near, low, 0.0))
    above, below = both_sides
    for p in range(4):
        for i in range(3):
            k, y, n = 4 * (3 * p + i), 4 * (3 * p + 1), 3 * p + i
            edge[n, 4:8, :] = above[y : y + 4] * above[k : k + 4]
            edge[n, 16:20, :] = below[y : y + 4] * below[k : k + 4]
    for p in range(4):
        for i in range(3):
            n = 3 * p + i
            top = base[p, i, 0:8]
            bottom = base[p, i, 8:16]
            for k, c in COEFS:
                top = top - c * edge[n, 8 - k : 16 - k, :]
                bottom = bottom + c * edge[n, 8 + k : 16 + k, :]
            base[p, i, 0:8] = top
            base[p, i, 8:16] = bottom

    l144, c256 = iota((ZROWS, 256), 0), iota((ZROWS, 256), 1)
    dist = jnp.where(l144 < 136, l144, l144 - ZROWS) - c256 // 2
    even = jnp.where(dist == 0, 45.0, jnp.where(dist == -1, -36.0, jnp.where(dist == 1, -8.0, jnp.where(dist == -2, -1.0, 0.0))))
    odd = jnp.where(dist == 1, 36.0, jnp.where(dist == 0, -45.0, jnp.where(dist == -1, 8.0, jnp.where(dist == 2, 1.0, 0.0))))
    along = jnp.where(c256 % 2 == 0, even, odd).astype(BF16)
    zrows = jnp.concatenate(
        [strs[p, s, 2:10, 0:ZROWS] for p in range(2) for s in Z_COMPS], 0
    )
    zder = mm2(zrows, along)
    for p in range(2):
        for i in range(3):
            r = 8 * (3 * p + i)
            for half in range(2):
                piece = zder[r : r + 8, 128 * half : 128 * half + 128]
                zd[p, i, half, pl.ds(0, 8, 2), :] = piece
                zd[p, i, half, pl.ds(1, 8, 2), :] = piece
    yder = []
    for p in range(2):
        for i, s in enumerate(Y_COMPS):
            c = {k: strs[p, s, 2 + k : 10 + k, 0:128] for k in range(-2, 3)}
            yder.append((
                45.0 * c[0] - 36.0 * c[-1] - 8.0 * c[1] - c[-2],
                36.0 * c[1] - 45.0 * c[0] + 8.0 * c[-1] + c[2],
            ))
    double = jnp.where(iota((128, 256), 1) // 2 == iota((128, 256), 0), 1.0, 0.0).astype(BF16)

    arrive(xstress)
    for i in range(3):
        c = [sland[0, 0, i], sland[0, 1, i], stx[0, i], stx[1, i], sland[1, 0, i], sland[1, 1, i]]
        for p in range(2):
            n = p + 2
            xder = (
                45.0 * c[n] - 36.0 * c[n - 1] - 8.0 * c[n + 1] - c[n - 2],
                36.0 * c[n + 1] - 45.0 * c[n] + 8.0 * c[n - 1] + c[n + 2],
            )
            for px in range(2):
                for py in range(2):
                    e2[2 * p + px, i, pl.ds(py, 8, 2), :] = xder[px] + yder[3 * p + i][py]
    fine = mm2(e2[...].reshape(192, 128), double)
    for p in range(4):
        for i in range(3):
            r = 16 * (3 * p + i)
            zpart = jnp.concatenate([zd[p // 2, i, 0], zd[p // 2, i, 1]], axis=1)
            total = base[p, i] + fine[r : r + 16] + zpart
            out[p, i] = vel[p, i] - (0.1 / 60.0) * total

    for copy, _ in copies:
        copy.wait_send()


def body(velocity, lift_weight, lift_bias, conv_weight, conv_bias, head_weight):
    vmem = pl.BlockSpec(memory_space=pltpu.VMEM)
    ncopies = 6 + 12 + 6 + 2 + 2 + 3 + 2 + 2 + 2
    scratch = [
        pltpu.VMEM((4, 3, 16, 256), F32),
        pltpu.VMEM((3, 32), F32),
        pltpu.VMEM((1, 32), F32),
        pltpu.VMEM((27, 8, 32), BF16),
        pltpu.VMEM((1, 8), BF16),
        pltpu.VMEM((6, 8), BF16),
        pltpu.VMEM((2, 96, 128), F32),
        pltpu.VMEM((2, 24, 128), F32),
        pltpu.VMEM((2, 2, 3, 4, 128), F32),
        pltpu.VMEM((2, 4, 128), F32),
        pltpu.VMEM((2, 3, 8, 128), F32),
        pltpu.VMEM((2, 48, 256), BF16),
        pltpu.VMEM((2, 48, 256), F32),
        pltpu.VMEM((4, 80, 128), F32),
        pltpu.VMEM((2, 4, 3, 4, 128), F32),
        pltpu.VMEM((3, 2, 3, 4, 128), F32),
        pltpu.VMEM((2, 24, 128), F32),
        pltpu.VMEM((2, 3, 8, 128), F32),
        pltpu.VMEM((2, 48, 256), BF16),
        pltpu.VMEM((2, 3, 3, 16, 256), F32),
        pltpu.VMEM((2, 3, 8, 128), F32),
        pltpu.VMEM((2, 2, 3, 8, 128), F32),
        pltpu.VMEM((4, 2 * ZROWS, 512), BF16),
        pltpu.VMEM((3, 384, 256), BF16),
        pltpu.VMEM((32, 128), F32),
        pltpu.VMEM((2, 6, 16, 256), F32),
        pltpu.VMEM((4, 3, 32, 256), F32),
        pltpu.VMEM((12, 24, 256), F32),
        pltpu.VMEM((4, 3, 16, 256), F32),
        pltpu.VMEM((4, 3, 16, 128), F32),
        pltpu.VMEM((2, 3, 2, 16, 128), F32),
        pltpu.SemaphoreType.DMA((ncopies,)),
        pltpu.SemaphoreType.DMA((ncopies,)),
        pltpu.SemaphoreType.DMA((6,)),
    ]
    return pl.pallas_call(
        body_kernel,
        out_shape=(
            jax.ShapeDtypeStruct((4, 3, 16, 256), F32),
            jax.ShapeDtypeStruct((2, 6, 8, 128), F32),
        ),
        in_specs=[pl.BlockSpec(memory_space=pltpu.HBM)] * 6,
        out_specs=(vmem, vmem),
        scratch_shapes=scratch,
        compiler_params=pltpu.CompilerParams(
            collective_id=0, has_side_effects=True, vmem_limit_bytes=40 * 2**20
        ),
    )(
        velocity,
        lift_weight.T,
        lift_bias.reshape(1, 32),
        conv_weight,
        conv_bias.reshape(1, 8),
        head_weight,
    )


def solution(mesh):
    placed = (
        P("chan", None, "row", "col"),
        P(),
        P(),
        P(None, "chan", None),
        P("chan"),
        P(None, "chan"),
    )
    return jax.shard_map(
        body,
        mesh=mesh,
        in_specs=placed,
        out_specs=(P("chan", None, "row", "col"), P("chan", None, "row", "col")),
        check_vma=False,
    )
```

time: 204 us -> 40.9 us (0.20)
  waiting for transfers between devices: 66.4 us -> 0 us
  starting transfers between devices: 60.1 us -> 0 us
  Pallas kernels: 0 us -> 36.2 us
  matrix products: 18.6 us -> 0 us
  local copies, waits for them, and re-layouts: 22 us -> 3.71 us
  between operations: 14.7 us -> 0.68 us
  blocking collectives: 10.2 us -> 0 us
  other arithmetic: 10.1 us -> 0 us
    ppermute x10 -> x0, starting transfers between devices: 60.1 us -> none  [the longest x5 42.2 us: padded_2(): lax.ppermute(tail, axis, [(i, (i + 1) % count) for i in range(count)])]
    ppermute x10 -> x0, waiting for transfers between devices: 39.3 us -> none  [the longest x5 27.9 us: padded_2(): lax.ppermute(head, axis, [((i + 1) % count, i) for i in range(count)])]
    pallas_call x0 -> x1, Pallas kernels: none -> 36.2 us  [body(): pl.pallas_call(body_kernel, out_shape=(jax.ShapeDtypeStruct((4, 3, 16, 25...]
    reduce_scatter x1 -> x0, waiting for transfers between devices: 27.1 us -> none  [body(): lax.psum_scatter(closure_rows(hidden, conv_weight, conv_bias, head_weight...]
    dot_general x29 -> x0, matrix products: 18.6 us -> none  [the longest x27 15.3 us: closure_rows(): jnp.einsum('oi,xiyz->xoyz', wide_weights[offset], piece, precision=lax.Pr...]
    reshape x2 -> x0, local copies, waits for them, and re-layouts: 15.1 us -> none  [the longest x1 14.7 us: coarsen(): velocity.reshape(nplanes // 2, 2, comps, ylen // 2, 2, zlen // 2, 2)]
    all_gather x1 -> x0, blocking collectives: 10.2 us -> none  [body(): gathered = lax.all_gather(box, 'chan', axis=0, tiled=True)]
    reduce_sum x1 -> x0, other arithmetic: 5.52 us -> none  [coarsen(): return jnp.mean(blocks, axis=(1, 4, 6))]
  transfers between devices with their start and end apart: 11 -> 0, of which waited for: 9 -> 0; matrix products, arithmetic and copies ran while one was open for 2% -> 0% of each run, Pallas kernels for 0% -> 0%
where the time goes in v1:
time: 40.9 us; the launch traced here: 40.6 us
  Pallas kernels  36.2 us (89%)
  local copies, waits for them, and re-layouts  3.71 us (9%)
  between operations  0.68 us (2%)
    pallas_call x1, Pallas kernels, body(): pl.pallas_call(body_kernel, out_shape=(jax.ShapeDtypeStruct((4, 3, 16, 25...  36.2 us
    unnamed x14, local copies, waits for them, and re-layouts  3.71 us

profile of v1, /device:TPU:1, one launch (start us, length us, event | category | flops | bytes accessed | tf_op | source)
XLA Modules:
  0.0 40.6 jit_solution(2753236670838165955)
XLA Ops:
  0.6 0.0 copy-start.3
  0.6 0.0 copy-start.2
  0.7 0.0 copy-start.4
  0.7 0.0 copy-start.5
  0.7 0.6 %copy-done.3 = bf16[6,8]{1,0:T(8,128)(2,1)S(1)} copy-done((bf16[6,8]{1,0:T(8,128)(2,1)S(1)}, bf16[6,8]{1,0:T(8,128)(2,1)}, u32[]{:S(2)}) %copy-start.3) | copy-done | bytes 120
  1.3 0.0 copy-done.2
  1.3 0.0 copy-done.4
  1.3 0.0 copy-done.5
  1.3 0.0 copy-start
  1.3 0.9 %copy-done = f32[4,3,16,256]{3,2,1,0:T(8,128)S(1)} copy-done((f32[4,3,16,256]{3,2,1,0:T(8,128)S(1)}, f32[4,3,16,256]{3,2,1,0:T(8,128)}, u32[]{:S(2)}) %copy-start) | copy-done | bytes 196632
  2.3 0.0 copy-start.1
  2.3 0.8 %copy-done.1 = bf16[27,8,32]{2,1,0:T(8,128)(2,1)S(1)} copy-done((bf16[27,8,32]{2,1,0:T(8,128)(2,1)S(1)}, bf16[27,8,32]{2,1,0:T(8,128)(2,1)}, u32[]{:S(2)}) %copy-start.1) | copy-done | bytes 13848
  3.1 36.2 %shard_map.77 = (f32[4,3,16,256]{3,2,1,0:T(8,128)S(1)}, f32[2,6,8,128]{3,2,1,0:T(8,128)S(1)}) custom-call(f32[4,3,16,256]{3,2,1,0:T(8,128)S(1)} %copy-done, f32[3,32]{1,0:T(4,128)S(1)} %bitcast.3, f32[1,32]{1,0:T(1,128)S(1)} %bitcast.4, bf16[27,8,32]{2,1,0:T(8,128)(2,1)S(1)} %copy-done.1, bf16[1,8]{1,0:T(2,128)(2,1)S(1)} %bitcast.5, bf16[6,8]{1,0:T(8,128)(2,1)S(1)} %copy-done.3), custom_call_target="tpu_custom_call" | custom-call | tf_op jit(solution)/shard_map/pallas_call | solution.py:462
  39.3 0.7 %copy.10 = f32[4,3,16,256]{3,2,1,0:T(8,128)} copy(f32[4,3,16,256]{3,2,1,0:T(8,128)S(1)} %get-tuple-element.4) | data formatting | bytes 393216
  40.0 0.6 %copy.11 = f32[2,6,8,128]{3,2,1,0:T(8,128)} copy(f32[2,6,8,128]{3,2,1,0:T(8,128)S(1)} %get-tuple-element.5) | data formatting | bytes 98304
Async XLA Ops:
  0.6 0.7 %copy-start.3 = (bf16[6,8]{1,0:T(8,128)(2,1)S(1)}, bf16[6,8]{1,0:T(8,128)(2,1)}, u32[]{:S(2)}) copy-start(bf16[6,8]{1,0:T(8,128)(2,1)} %head_w_in.1) | copy-start | bytes 292
  0.6 0.7 %copy-start.2 = (f32[32,3]{0,1:T(4,128)S(1)}, f32[32,3]{0,1:T(4,128)}, u32[]{:S(2)}) copy-start(f32[32,3]{0,1:T(4,128)} %param.7) | copy-start | bytes 1156
  0.7 0.7 %copy-start.4 = (f32[32]{0:T(128)S(1)}, f32[32]{0:T(128)}, u32[]{:S(2)}) copy-start(f32[32]{0:T(128)} %param.8) | copy-start | bytes 388
  0.7 0.7 %copy-start.5 = (bf16[8]{0:T(256)(128)(2,1)S(1)}, bf16[8]{0:T(256)(128)(2,1)}, u32[]{:S(2)}) copy-start(bf16[8]{0:T(256)(128)(2,1)} %param.10) | copy-start | bytes 52
  1.3 0.9 %copy-start = (f32[4,3,16,256]{3,2,1,0:T(8,128)S(1)}, f32[4,3,16,256]{3,2,1,0:T(8,128)}, u32[]{:S(2)}) copy-start(f32[4,3,16,256]{3,2,1,0:T(8,128)} %vel_in.1) | copy-start | bytes 589828
  2.3 0.8 %copy-start.1 = (bf16[27,8,32]{2,1,0:T(8,128)(2,1)S(1)}, bf16[27,8,32]{2,1,0:T(8,128)(2,1)}, u32[]{:S(2)}) copy-start(bf16[27,8,32]{2,1,0:T(8,128)(2,1)} %conv_w_in.1) | copy-start | bytes 41476

commit v2 on v1

--- a/solution.py
+++ b/solution.py
@@ -15,13 +15,8 @@
 Y_COMPS = (3, 1, 5)
 Z_COMPS = (4, 5, 2)
 
-PEERS = [
-    (dr, dc, dx)
-    for dr in (-1, 0, 1)
-    for dc in (-1, 0, 1)
-    for dx in (-1, 0, 1)
-    if (dr, dc, dx) != (0, 0, 0)
-] + [(0, 0, 2)]
+NEAR = [(0, dc, dx) for dc in (-1, 0, 1) for dx in (-1, 0, 1) if (dc, dx) != (0, 0)] + [(0, 0, 2)]
+FAR = [(dr, dc, dx) for dr in (-1, 1) for dc in (-1, 0, 1) for dx in (-1, 0, 1)]
 
 
 def iota(shape, dim):
@@ -75,7 +70,7 @@
     xs, bx, ysend, csend, zvsend, yvsend, yvstage, wall,
     yland, cland, xland, zvland, yvland, xv, stx, sland,
     hid, taps, headk, strs, field, edge, base, e2, zd,
-    send_sem, recv_sem, load_sem,
+    send_sem, recv_sem, load_sem, ready,
 ):
     here = (lax.axis_index("row"), lax.axis_index("col"), lax.axis_index("chan"))
     me = here[2]
@@ -86,9 +81,16 @@
             for h, o, n in zip(here, off, (NROW, NCOL, NCHAN))
         )
 
+    odd = lax.rem(here[0], 2)
     barrier = pltpu.get_barrier_semaphore()
-    for off in PEERS:
+    for off in NEAR:
         pl.semaphore_signal(barrier, inc=1, device_id=peer(off), device_id_type=MESH)
+
+    @pl.when(odd == 0)
+    def _():
+        for off in FAR:
+            pl.semaphore_signal(barrier, inc=1, device_id=peer(off), device_id_type=MESH)
+
 
     pairs_in = (
         (vel_in, vel), (conv_w_in, conv_w), (lift_w_in, lift_w), (lift_b_in, lift_b),
@@ -101,13 +103,14 @@
         load.start()
     copies = []
 
-    def send(src, dst, source, landed=None):
+    def send(src, dst, source, landed=None, start=True):
         k = len(copies)
         copy = pltpu.make_async_remote_copy(
             src_ref=src, dst_ref=dst, send_sem=send_sem.at[k], recv_sem=recv_sem.at[k],
             device_id=peer(tuple(-s for s in source)), device_id_type=MESH,
         )
-        copy.start()
+        if start:
+            copy.start()
         if landed is not None:
             copies.append((copy, pltpu.make_async_remote_copy(
                 src_ref=src, dst_ref=landed, send_sem=send_sem.at[k], recv_sem=recv_sem.at[k],
@@ -158,24 +161,34 @@
         moved = pltpu.roll(low.astype(F32), (spare - near) % 48, 0)
         yvsend[s] = jnp.where(slot == spare, moved, high.astype(F32)).astype(BF16)
 
-    pl.semaphore_wait(barrier, len(PEERS))
+    pl.semaphore_wait(barrier, len(NEAR) + len(FAR) * odd)
 
     ybox, corner, ycols, yvel = [], [], [], []
     for s, dr in ((0, -1), (1, 1)):
-        ybox.append(send(ysend.at[s], yland.at[s, 1:3], (dr, 0, 0)))
-    for s, dr in ((0, -1), (1, 1)):
-        ybox.append(send(ysend.at[s, 1], yland.at[s, 0], (dr, 0, -1)))
-        ybox.append(send(ysend.at[s, 0], yland.at[s, 3], (dr, 0, 1)))
+        ybox.append(send(ysend.at[s], yland.at[s, 1:3], (dr, 0, 0), start=False))
+        ybox.append(send(ysend.at[s, 1], yland.at[s, 0], (dr, 0, -1), start=False))
+        ybox.append(send(ysend.at[s, 0], yland.at[s, 3], (dr, 0, 1), start=False))
     for s, dr in ((1, -1), (2, 1)):
         for t, dc in ((0, -1), (1, 1)):
             for dx in (-1, 0, 1):
-                corner.append(send(csend.at[t], cland.at[s, t, dx + 1], (dr, dc, dx)))
+                corner.append(
+                    send(csend.at[t], cland.at[s, t, dx + 1], (dr, dc, dx), start=False)
+                )
+    for s, dr in ((0, -1), (1, 1)):
+        yvel.append(send(yvsend.at[s], yvland.at[s], (dr, 0, 0), start=False))
+    far_copies = [copies[k][0] for k in ybox + corner + yvel]
+
+    @pl.when(odd == 1)
+    def _():
+        for copy in far_copies:
+            copy.start()
+        for off in FAR:
+            pl.semaphore_signal(ready, inc=1, device_id=peer(off), device_id_type=MESH)
+
     for t, dc in ((0, -1), (1, 1)):
         for dx in (-1, 0, 1):
             ycols.append(send(csend.at[t], cland.at[0, t, dx + 1], (0, dc, dx)))
     xbox = [send(bx.at[1], xland.at[0], (0, 0, -1)), send(bx.at[0], xland.at[1], (0, 0, 1))]
-    for s, dr in ((0, -1), (1, 1)):
-        yvel.append(send(yvsend.at[s], yvland.at[s], (dr, 0, 0)))
 
     for load in loads[1:]:
         load.wait()
@@ -319,6 +332,12 @@
             for k, c in COEFS:
                 total = total + c * (planes[p + 3 + k] - planes[p + 3 - k])
             base[p, i] = total
+
+    @pl.when(odd == 0)
+    def _():
+        pl.semaphore_wait(ready, len(FAR))
+        for copy in far_copies:
+            copy.start()
 
     arrive(ybox)
     for q in range(4):
@@ -458,6 +477,7 @@
         pltpu.SemaphoreType.DMA((ncopies,)),
         pltpu.SemaphoreType.DMA((ncopies,)),
         pltpu.SemaphoreType.DMA((6,)),
+        pltpu.SemaphoreType.REGULAR,
     ]
     return pl.pallas_call(
         body_kernel,
@@ -469,7 +489,7 @@
         out_specs=(vmem, vmem),
         scratch_shapes=scratch,
         compiler_params=pltpu.CompilerParams(
-            collective_id=0, has_side_effects=True, vmem_limit_bytes=40 * 2**20
+            collective_id=0, has_side_effects=True, vmem_limit_bytes=60 * 2**20
         ),
     )(
         velocity,

time: 40.9 us -> 37.5 us (0.917)
  Pallas kernels: 36.2 us -> 34.4 us
  local copies, waits for them, and re-layouts: 3.71 us -> 2.25 us
    pallas_call x1, Pallas kernels: 36.2 us -> 34.4 us  [body(): pl.pallas_call(body_kernel, out_shape=(jax.ShapeDtypeStruct((4, 3, 16, 25...]
    unnamed x14 -> x4, local copies, waits for them, and re-layouts: 3.71 us -> 2.25 us
where the time goes in v2:
time: 37.5 us; the launch traced here: 37.3 us
  Pallas kernels  34.4 us (92%)
  local copies, waits for them, and re-layouts  2.25 us (6%)
  between operations  0.65 us (2%)
    pallas_call x1, Pallas kernels, body(): pl.pallas_call(body_kernel, out_shape=(jax.ShapeDtypeStruct((4, 3, 16, 25...  34.4 us
    unnamed x4, local copies, waits for them, and re-layouts  2.25 us

profile of v2, /device:TPU:1, one launch (start us, length us, event | category | flops | bytes accessed | tf_op | source)
XLA Modules:
  0.0 37.3 jit_solution(9337501160928344355)
XLA Ops:
  0.6 34.4 %shard_map.77 = (f32[4,3,16,256]{3,2,1,0:T(8,128)}, f32[2,6,8,128]{3,2,1,0:T(8,128)}) custom-call(f32[4,3,16,256]{3,2,1,0:T(8,128)} %vel_in.1, f32[3,32]{1,0:T(4,128)} %bitcast.3, f32[1,32]{1,0:T(1,128)} %bitcast.4, bf16[27,8,32]{2,1,0:T(8,128)(2,1)} %conv_w_in.1, bf16[1,8]{1,0:T(2,128)(2,1)} %bitcast.5, bf16[6,8]{1,0:T(8,128)(2,1)} %head_w_in.1), custom_call_target="tpu_custom_call" | custom-call | tf_op jit(solution)/shard_map/pallas_call | solution.py:482
  35.1 0.0 copy-start
  35.1 1.6 %copy.10 = f32[4,3,16,256]{3,2,1,0:T(8,128)} copy(f32[4,3,16,256]{3,2,1,0:T(8,128)} %get-tuple-element.4) | data formatting | bytes 393216
  36.7 0.0 copy-done
  36.7 0.6 %copy.11 = f32[2,6,8,128]{3,2,1,0:T(8,128)} copy(f32[2,6,8,128]{3,2,1,0:T(8,128)S(1)} %copy-done) | data formatting | bytes 98304
Async XLA Ops:
  35.1 1.6 %copy-start = (f32[2,6,8,128]{3,2,1,0:T(8,128)S(1)}, f32[2,6,8,128]{3,2,1,0:T(8,128)}, u32[]{:S(2)}) copy-start(f32[2,6,8,128]{3,2,1,0:T(8,128)} %get-tuple-element.5) | copy-start | bytes 147460

commit v3 on v2

--- a/solution.py
+++ b/solution.py
@@ -16,6 +16,7 @@
 Z_COMPS = (4, 5, 2)
 
 NEAR = [(0, dc, dx) for dc in (-1, 0, 1) for dx in (-1, 0, 1) if (dc, dx) != (0, 0)] + [(0, 0, 2)]
+BEYOND = [(0, 1, dx) for dx in (-1, 0, 1)]
 FAR = [(dr, dc, dx) for dr in (-1, 1) for dc in (-1, 0, 1) for dx in (-1, 0, 1)]
 
 
@@ -63,14 +64,30 @@
     return total.astype(BF16)
 
 
+NEAREST, SPARE = (3, 0), (0, 3)
+
+
+def packed(rows, s):
+    high, low = split(rows)
+    moved = pltpu.roll(low.astype(F32), (SPARE[s] - NEAREST[s]) % rows.shape[0], 0)
+    slot = iota(rows.shape, 0) % 4
+    return jnp.where(slot == SPARE[s], moved, high.astype(F32)).astype(BF16)
+
+
+def unpacked(rows, s):
+    rows = rows.astype(F32)
+    low = pltpu.roll(rows, (NEAREST[s] - SPARE[s]) % rows.shape[0], 0)
+    return rows + jnp.where(iota(rows.shape, 0) % 4 == NEAREST[s], low, 0.0)
+
+
 def body_kernel(
     vel_in, lift_w_in, lift_b_in, conv_w_in, conv_b_in, head_w_in,
     out, stress_out,
     vel, lift_w, lift_b, conv_w, conv_b, head_w,
-    xs, bx, ysend, csend, zvsend, yvsend, yvstage, wall,
+    xs, bx, ystage, ydec, ysend, csend, zvsend, yvsend, yvstage, wall,
     yland, cland, xland, zvland, yvland, xv, stx, sland,
     hid, taps, headk, strs, field, edge, base, e2, zd,
-    send_sem, recv_sem, load_sem, ready,
+    send_sem, recv_sem, load_sem, ready, wrapped,
 ):
     here = (lax.axis_index("row"), lax.axis_index("col"), lax.axis_index("chan"))
     me = here[2]
@@ -82,9 +99,16 @@
         )
 
     odd = lax.rem(here[0], 2)
+    leftmost, rightmost = here[1] == 0, here[1] == NCOL - 1
     barrier = pltpu.get_barrier_semaphore()
     for off in NEAR:
-        pl.semaphore_signal(barrier, inc=1, device_id=peer(off), device_id_type=MESH)
+        if off[1] < 1:
+            pl.semaphore_signal(barrier, inc=1, device_id=peer(off), device_id_type=MESH)
+
+    @pl.when(jnp.logical_not(rightmost))
+    def _():
+        for off in BEYOND:
+            pl.semaphore_signal(barrier, inc=1, device_id=peer(off), device_id_type=MESH)
 
     @pl.when(odd == 0)
     def _():
@@ -129,6 +153,7 @@
     ends = jnp.where(r16 < 4, r16, r16 + 120)
     picker = jnp.where((iota((16, 256), 1) // 2 == ends) & (r16 < 8), 1.0, 0.0).astype(BF16)
     csend[...] = jnp.zeros_like(csend)
+    ystage[...] = jnp.zeros_like(ystage)
     loads[0].wait()
     for p in range(2):
         for c in range(3):
@@ -147,21 +172,27 @@
     for p in range(2):
         for c in range(3):
             r = 8 * (3 * p + c)
-            ysend[0, p, c] = box[r + 4 : r + 8]
-            ysend[1, p, c] = box[r : r + 4]
+            ystage[0, 16 * p + 4 * c : 16 * p + 4 * c + 4, :] = box[r + 4 : r + 8]
+            ystage[1, 16 * p + 4 * c : 16 * p + 4 * c + 4, :] = box[r : r + 4]
+    for s in range(2):
+        ysend[s] = packed(ystage[s], s).reshape(2, 16, 128)
     columns = mm(picker, pieces[0], NT) + mm(picker, pieces[1], NT) + mm(picker, pieces[2], NT)
     csend[0, :, 0:48] = columns[4:8]
     csend[1, :, 0:48] = columns[0:4]
     for k in range(12):
         yvstage[0, 4 * k : 4 * k + 4, :] = vel[k // 3, k % 3, 12:16, :]
         yvstage[1, 4 * k : 4 * k + 4, :] = vel[k // 3, k % 3, 0:4, :]
-    slot = iota((48, 256), 0) % 4
-    for s, near, spare in ((0, 3, 0), (1, 0, 3)):
-        high, low = split(yvstage[s])
-        moved = pltpu.roll(low.astype(F32), (spare - near) % 48, 0)
-        yvsend[s] = jnp.where(slot == spare, moved, high.astype(F32)).astype(BF16)
-
-    pl.semaphore_wait(barrier, len(NEAR) + len(FAR) * odd)
+    for s in range(2):
+        yvsend[s] = packed(yvstage[s], s)
+
+    pl.semaphore_wait(
+        barrier, len(NEAR) - jnp.where(leftmost, len(BEYOND), 0) + len(FAR) * odd
+    )
+
+    @pl.when(rightmost)
+    def _():
+        for off in BEYOND:
+            pl.semaphore_signal(wrapped, inc=1, device_id=peer(off), device_id_type=MESH)
 
     ybox, corner, ycols, yvel = [], [], [], []
     for s, dr in ((0, -1), (1, 1)):
@@ -176,18 +207,28 @@
                 )
     for s, dr in ((0, -1), (1, 1)):
         yvel.append(send(yvsend.at[s], yvland.at[s], (dr, 0, 0), start=False))
-    far_copies = [copies[k][0] for k in ybox + corner + yvel]
+    far_copies = [copies[k][0] for k in ybox + corner]
+    late_copies = [copies[k][0] for k in yvel]
 
     @pl.when(odd == 1)
     def _():
-        for copy in far_copies:
-            copy.start()
         for off in FAR:
             pl.semaphore_signal(ready, inc=1, device_id=peer(off), device_id_type=MESH)
+        for copy in far_copies:
+            copy.start()
 
     for t, dc in ((0, -1), (1, 1)):
         for dx in (-1, 0, 1):
-            ycols.append(send(csend.at[t], cland.at[0, t, dx + 1], (0, dc, dx)))
+            ycols.append(
+                send(csend.at[t], cland.at[0, t, dx + 1], (0, dc, dx), start=dc == -1)
+            )
+    left_copies = [copies[k][0] for k in ycols[3:]]
+
+    @pl.when(jnp.logical_not(leftmost))
+    def _():
+        for copy in left_copies:
+            copy.start()
+
     xbox = [send(bx.at[1], xland.at[0], (0, 0, -1)), send(bx.at[0], xland.at[1], (0, 0, 1))]
 
     for load in loads[1:]:
@@ -211,7 +252,14 @@
         cols = mm(take, vel[:, c].reshape(64, 256), NT, exact=True)
         zvsend[0, c, :, 0:64] = cols[0:8]
         zvsend[1, c, :, 0:64] = cols[8:16]
-    zvel = [send(zvsend.at[t], zvland.at[t], (0, dc, 0)) for t, dc in ((0, -1), (1, 1))]
+    zvel = [
+        send(zvsend.at[t], zvland.at[t], (0, dc, 0), start=dc == -1) for t, dc in ((0, -1), (1, 1))
+    ]
+
+    @pl.when(jnp.logical_not(leftmost))
+    def _():
+        copies[zvel[1]][0].start()
+
     xvel = [send(vel.at[1:4], xv.at[0], (0, 0, -1)), send(vel.at[0:3], xv.at[1], (0, 0, 1))]
 
     spread = jnp.where(iota((32, 256), 1) % 32 == iota((32, 256), 0), 1.0, 0.0)
@@ -262,6 +310,12 @@
             r = 128 * c + 32 * y
             taps[a, r : r + 32, 0:128] = first.astype(BF16)
             taps[a, r : r + 32, 128:256] = second.astype(BF16)
+
+    @pl.when(odd == 1)
+    def _():
+        for copy in late_copies:
+            copy.start()
+
     params = wall[0, 72:80, :]
     for n in range(1, 4):
         params = params + pltpu.roll(wall[n, 72:80, :], 8 * n, 1)
@@ -270,6 +324,12 @@
     for n in range(4):
         headk[pl.ds(n, 8, 4), :] = rolled[n]
     head = headk[...].astype(BF16)
+
+    @pl.when(leftmost)
+    def _():
+        pl.semaphore_wait(wrapped, len(BEYOND))
+        for copy in left_copies + [copies[zvel[1]][0]]:
+            copy.start()
 
     arrive(ycols)
     for q, dx, p in PLANES:
@@ -340,9 +400,17 @@
             copy.start()
 
     arrive(ybox)
+
+    @pl.when(odd == 0)
+    def _():
+        for copy in late_copies:
+            copy.start()
+
+    for s in range(2):
+        ydec[s] = unpacked(yland[s].reshape(64, 128), s)
     for q in range(4):
         rows = jnp.concatenate(
-            [jnp.concatenate([yland[1, q, c], yland[0, q, c]], 0) for c in range(3)], 0
+            [ydec[s, 16 * q + 4 * c : 16 * q + 4 * c + 4, :] for c in range(3) for s in (1, 0)], 0
         )
         h = lifted(rows)
         hold(q, 0, 0, h[:, 128:256])
@@ -367,12 +435,7 @@
 
     arrive(yvel)
     edge[...] = jnp.zeros_like(edge)
-    both_sides = []
-    for s, near, spare in ((0, 3, 0), (1, 0, 3)):
-        rows = yvland[s].astype(F32)
-        low = pltpu.roll(rows, (near - spare) % 48, 0)
-        both_sides.append(rows + jnp.where(slot == near, low, 0.0))
-    above, below = both_sides
+    above, below = (unpacked(yvland[s], s) for s in range(2))
     for p in range(4):
         for i in range(3):
             k, y, n = 4 * (3 * p + i), 4 * (3 * p + 1), 3 * p + i
@@ -451,13 +514,15 @@
         pltpu.VMEM((6, 8), BF16),
         pltpu.VMEM((2, 96, 128), F32),
         pltpu.VMEM((2, 24, 128), F32),
-        pltpu.VMEM((2, 2, 3, 4, 128), F32),
+        pltpu.VMEM((2, 32, 128), F32),
+        pltpu.VMEM((2, 64, 128), F32),
+        pltpu.VMEM((2, 2, 16, 128), BF16),
         pltpu.VMEM((2, 4, 128), F32),
         pltpu.VMEM((2, 3, 8, 128), F32),
         pltpu.VMEM((2, 48, 256), BF16),
         pltpu.VMEM((2, 48, 256), F32),
         pltpu.VMEM((4, 80, 128), F32),
-        pltpu.VMEM((2, 4, 3, 4, 128), F32),
+        pltpu.VMEM((2, 4, 16, 128), BF16),
         pltpu.VMEM((3, 2, 3, 4, 128), F32),
         pltpu.VMEM((2, 24, 128), F32),
         pltpu.VMEM((2, 3, 8, 128), F32),
@@ -478,12 +543,13 @@
         pltpu.SemaphoreType.DMA((ncopies,)),
         pltpu.SemaphoreType.DMA((6,)),
         pltpu.SemaphoreType.REGULAR,
+        pltpu.SemaphoreType.REGULAR,
     ]
     return pl.pallas_call(
         body_kernel,
         out_shape=(
-            jax.ShapeDtypeStruct((4, 3, 16, 256), F32),
-            jax.ShapeDtypeStruct((2, 6, 8, 128), F32),
+            pltpu.VMEM((4, 3, 16, 256), F32),
+            pltpu.VMEM((2, 6, 8, 128), F32),
         ),
         in_specs=[pl.BlockSpec(memory_space=pltpu.HBM)] * 6,
         out_specs=(vmem, vmem),

time: 37.5 us -> 32.7 us (0.87)
  Pallas kernels: 34.4 us -> 30.6 us
  local copies, waits for them, and re-layouts: 2.25 us -> 1.3 us
    pallas_call x1, Pallas kernels: 34.4 us -> 30.6 us  [body(): pl.pallas_call(body_kernel, out_shape=(pltpu.VMEM((4, 3, 16, 256), F32),...]
    unnamed x4 -> x2, local copies, waits for them, and re-layouts: 2.25 us -> 1.3 us
where the time goes in v3:
time: 32.7 us; the launch traced here: 32.5 us
  Pallas kernels  30.6 us (94%)
  local copies, waits for them, and re-layouts  1.3 us (4%)
  between operations  0.64 us (2%)
    pallas_call x1, Pallas kernels, body(): pl.pallas_call(body_kernel, out_shape=(pltpu.VMEM((4, 3, 16, 256), F32),...  30.6 us
    unnamed x2, local copies, waits for them, and re-layouts  1.3 us

profile of v3, /device:TPU:1, one launch (start us, length us, event | category | flops | bytes accessed | tf_op | source)
XLA Modules:
  0.0 32.5 jit_solution(17836306538745371234)
XLA Ops:
  0.6 30.6 %shard_map.77 = (f32[4,3,16,256]{3,2,1,0:T(8,128)S(1)}, f32[2,6,8,128]{3,2,1,0:T(8,128)S(1)}) custom-call(f32[4,3,16,256]{3,2,1,0:T(8,128)} %vel_in.1, f32[3,32]{1,0:T(4,128)} %bitcast.3, f32[1,32]{1,0:T(1,128)} %bitcast.4, bf16[27,8,32]{2,1,0:T(8,128)(2,1)} %conv_w_in.1, bf16[1,8]{1,0:T(2,128)(2,1)} %bitcast.5, bf16[6,8]{1,0:T(8,128)(2,1)} %head_w_in.1), custom_call_target="tpu_custom_call" | custom-call | tf_op jit(solution)/shard_map/pallas_call | solution.py:548
  31.2 0.7 %copy.10 = f32[4,3,16,256]{3,2,1,0:T(8,128)} copy(f32[4,3,16,256]{3,2,1,0:T(8,128)S(1)} %get-tuple-element.2) | data formatting | bytes 393216
  31.9 0.6 %copy.11 = f32[2,6,8,128]{3,2,1,0:T(8,128)} copy(f32[2,6,8,128]{3,2,1,0:T(8,128)S(1)} %get-tuple-element.3) | data formatting | bytes 98304

commit v4 on v3

--- a/solution.py
+++ b/solution.py
@@ -80,13 +80,21 @@
     return rows + jnp.where(iota(rows.shape, 0) % 4 == NEAREST[s], low, 0.0)
 
 
+def skewed(rows, start, step):
+    turn = iota(rows.shape, 0) % 4
+    total = pltpu.roll(rows, start % 128, 1) if start % 128 else rows
+    for n in range(1, 4):
+        total = jnp.where(turn == n, pltpu.roll(rows, (start + step * n) % 128, 1), total)
+    return total
+
+
 def body_kernel(
     vel_in, lift_w_in, lift_b_in, conv_w_in, conv_b_in, head_w_in,
     out, stress_out,
     vel, lift_w, lift_b, conv_w, conv_b, head_w,
     xs, bx, ystage, ydec, ysend, csend, zvsend, yvsend, yvstage, wall,
-    yland, cland, xland, zvland, yvland, xv, stx, sland,
-    hid, taps, headk, strs, field, edge, base, e2, zd,
+    yland, cland, cpack, cfar, cwide, xland, zvland, yvland, xv, stx, sland,
+    hid, taps, early, headk, strs, field, edge, base, e2, zd,
     send_sem, recv_sem, load_sem, ready, wrapped,
 ):
     here = (lax.axis_index("row"), lax.axis_index("col"), lax.axis_index("chan"))
@@ -179,6 +187,17 @@
     columns = mm(picker, pieces[0], NT) + mm(picker, pieces[1], NT) + mm(picker, pieces[2], NT)
     csend[0, :, 0:48] = columns[4:8]
     csend[1, :, 0:48] = columns[0:4]
+    ends8 = csend[...].reshape(8, 128)
+    lane8 = iota((8, 128), 1)
+    for p in range(2):
+        mine = jnp.where((lane8 >= 24 * p) & (lane8 < 24 * p + 24), ends8, 0.0)
+        spaced = skewed(mine, 128 - 24 * p, 32)
+        for t in range(2):
+            row = spaced[4 * t : 4 * t + 1]
+            for n in range(1, 4):
+                row = row + spaced[4 * t + n : 4 * t + n + 1]
+            cpack[t, p] = row
+    cwide[...] = jnp.zeros_like(cwide)
     for k in range(12):
         yvstage[0, 4 * k : 4 * k + 4, :] = vel[k // 3, k % 3, 12:16, :]
         yvstage[1, 4 * k : 4 * k + 4, :] = vel[k // 3, k % 3, 0:4, :]
@@ -199,12 +218,13 @@
         ybox.append(send(ysend.at[s], yland.at[s, 1:3], (dr, 0, 0), start=False))
         ybox.append(send(ysend.at[s, 1], yland.at[s, 0], (dr, 0, -1), start=False))
         ybox.append(send(ysend.at[s, 0], yland.at[s, 3], (dr, 0, 1), start=False))
-    for s, dr in ((1, -1), (2, 1)):
+    for s, dr in ((0, -1), (1, 1)):
         for t, dc in ((0, -1), (1, 1)):
-            for dx in (-1, 0, 1):
-                corner.append(
-                    send(csend.at[t], cland.at[s, t, dx + 1], (dr, dc, dx), start=False)
-                )
+            corner += [
+                send(cpack.at[t, 1], cfar.at[s, t, 0], (dr, dc, -1), start=False),
+                send(cpack.at[t], cfar.at[s, t, 1:3], (dr, dc, 0), start=False),
+                send(cpack.at[t, 0], cfar.at[s, t, 3], (dr, dc, 1), start=False),
+            ]
     for s, dr in ((0, -1), (1, 1)):
         yvel.append(send(yvsend.at[s], yvland.at[s], (dr, 0, 0), start=False))
     far_copies = [copies[k][0] for k in ybox + corner]
@@ -220,7 +240,7 @@
     for t, dc in ((0, -1), (1, 1)):
         for dx in (-1, 0, 1):
             ycols.append(
-                send(csend.at[t], cland.at[0, t, dx + 1], (0, dc, dx), start=dc == -1)
+                send(csend.at[t], cland.at[t, dx + 1], (0, dc, dx), start=dc == -1)
             )
     left_copies = [copies[k][0] for k in ycols[3:]]
 
@@ -281,9 +301,9 @@
     def lifted(rows):
         return jnp.tanh(mm(rows, lift, TN, exact=True) + bias)
 
-    def side(s, dx):
+    def side(dx):
         return jnp.concatenate(
-            [cland[s, 1, dx + 1], jnp.zeros((8, 128), F32), cland[s, 0, dx + 1]], 0
+            [cland[1, dx + 1], jnp.zeros((8, 128), F32), cland[0, dx + 1]], 0
         )
 
     PLANES = ((0, -1, 1), (1, 0, 0), (2, 0, 1), (3, 1, 0))
@@ -308,8 +328,9 @@
         )
         for y, (first, second) in enumerate(tiles):
             r = 128 * c + 32 * y
-            taps[a, r : r + 32, 0:128] = first.astype(BF16)
-            taps[a, r : r + 32, 128:256] = second.astype(BF16)
+            for h, half in enumerate((first, second)):
+                taps[h, a, r : r + 32, 0:128] = half.astype(BF16)
+                taps[h, a, r : r + 32, 128:256] = half.astype(BF16)
 
     @pl.when(odd == 1)
     def _():
@@ -333,17 +354,20 @@
 
     arrive(ycols)
     for q, dx, p in PLANES:
-        hold(q, 128, 128, jnp.tanh(mm(side(0, dx), lift_of[p], exact=True) + bias))
-
-    def closure(g):
+        hold(q, 128, 128, jnp.tanh(mm(side(dx), lift_of[p], exact=True) + bias))
+
+    def partial(h, tile):
         total = None
         for a in range(3):
-            block = hid[a : a + 2, :, 128 * g : 128 * g + 256].reshape(4 * ZROWS, 256)
-            term = mm(block, taps[a], NT)
+            block = [hid[a : a + 2, n : n + ZROWS, 128 * tile : 128 * tile + 128] for n in (0, ZROWS)]
+            block = jnp.concatenate(block, axis=2).reshape(2 * ZROWS, 256)
+            term = mm(block, taps[h, a], NT)
             total = term if total is None else total + term
+        return total
+
+    def closure(g, total):
         for p in range(2):
-            r = 2 * ZROWS * p
-            both = total[r : r + ZROWS] + total[r + ZROWS : r + 2 * ZROWS]
+            both = total[ZROWS * p : ZROWS * p + ZROWS]
             conv = (
                 pltpu.roll(both[:, 0:128], 1, 0)
                 + both[:, 128:256]
@@ -356,7 +380,9 @@
             for s in range(6):
                 strs[p, s, 4 * g : 4 * g + 4, 0:ZROWS] = found[4 * s : 4 * s + 4]
 
-    closure(1)
+    closure(1, partial(0, 1) + partial(1, 2))
+    early[0] = partial(1, 1)
+    early[1] = partial(0, 2)
 
     field[...] = jnp.zeros_like(field)
     for p in range(4):
@@ -416,13 +442,18 @@
         hold(q, 0, 0, h[:, 128:256])
         hold(q, 0, 384, h[:, 0:128])
     arrive(corner)
-    for q, dx, p in PLANES:
-        rows = jnp.concatenate([side(1, dx), side(2, dx)], 0)
-        h = jnp.tanh(mm(rows, lift_of[p], exact=True) + bias)
-        hold(q, 128, 0, h[0:16, 128:256])
-        hold(q, 128, 384, h[16:32, 0:128])
-    closure(0)
-    closure(2)
+    for q in range(4):
+        for s in range(2):
+            r = 16 * (2 * q + s)
+            cwide[r : r + 4, :] = jnp.broadcast_to(cfar[s, 1, q], (4, 128))
+            cwide[r + 12 : r + 16, :] = jnp.broadcast_to(cfar[s, 0, q], (4, 128))
+    rows = skewed(cwide[...], 128, 96)
+    h = jnp.tanh(mm(rows, lift_of[0], exact=True) + bias)
+    for q in range(4):
+        hold(q, 128, 0, h[32 * q : 32 * q + 16, 128:256])
+        hold(q, 128, 384, h[32 * q + 16 : 32 * q + 32, 0:128])
+    closure(0, early[0] + partial(0, 0))
+    closure(2, early[1] + partial(1, 3))
 
     for p in range(2):
         for i, s in enumerate(X_COMPS):
@@ -523,7 +554,10 @@
         pltpu.VMEM((2, 48, 256), F32),
         pltpu.VMEM((4, 80, 128), F32),
         pltpu.VMEM((2, 4, 16, 128), BF16),
-        pltpu.VMEM((3, 2, 3, 4, 128), F32),
+        pltpu.VMEM((2, 3, 4, 128), F32),
+        pltpu.VMEM((2, 2, 1, 128), F32),
+        pltpu.VMEM((2, 2, 4, 1, 128), F32),
+        pltpu.VMEM((128, 128), F32),
         pltpu.VMEM((2, 24, 128), F32),
         pltpu.VMEM((2, 3, 8, 128), F32),
         pltpu.VMEM((2, 48, 256), BF16),
@@ -531,7 +565,8 @@
         pltpu.VMEM((2, 3, 8, 128), F32),
         pltpu.VMEM((2, 2, 3, 8, 128), F32),
         pltpu.VMEM((4, 2 * ZROWS, 512), BF16),
-        pltpu.VMEM((3, 384, 256), BF16),
+        pltpu.VMEM((2, 3, 384, 256), BF16),
+        pltpu.VMEM((2, 2 * ZROWS, 384), F32),
         pltpu.VMEM((32, 128), F32),
         pltpu.VMEM((2, 6, 16, 256), F32),
         pltpu.VMEM((4, 3, 32, 256), F32),

time: 32.7 us -> 32.4 us (level)
  no operation moved by 1% of the time
where the time goes in v4:
time: 32.4 us; the launch traced here: 32.2 us
  Pallas kernels  30.3 us (94%)
  local copies, waits for them, and re-layouts  1.3 us (4%)
  between operations  0.64 us (2%)
    pallas_call x1, Pallas kernels, body(): pl.pallas_call(body_kernel, out_shape=(pltpu.VMEM((4, 3, 16, 256), F32),...  30.3 us
    unnamed x2, local copies, waits for them, and re-layouts  1.3 us

profile of v4, /device:TPU:1, one launch (start us, length us, event | category | flops | bytes accessed | tf_op | source)
XLA Modules:
  0.0 32.2 jit_solution(3262234398846539757)
XLA Ops:
  0.6 30.3 %shard_map.77 = (f32[4,3,16,256]{3,2,1,0:T(8,128)S(1)}, f32[2,6,8,128]{3,2,1,0:T(8,128)S(1)}) custom-call(f32[4,3,16,256]{3,2,1,0:T(8,128)} %vel_in.1, f32[3,32]{1,0:T(4,128)} %bitcast.3, f32[1,32]{1,0:T(1,128)} %bitcast.4, bf16[27,8,32]{2,1,0:T(8,128)(2,1)} %conv_w_in.1, bf16[1,8]{1,0:T(2,128)(2,1)} %bitcast.5, bf16[6,8]{1,0:T(8,128)(2,1)} %head_w_in.1), custom_call_target="tpu_custom_call" | custom-call | tf_op jit(solution)/shard_map/pallas_call | solution.py:583
  30.9 0.7 %copy.10 = f32[4,3,16,256]{3,2,1,0:T(8,128)} copy(f32[4,3,16,256]{3,2,1,0:T(8,128)S(1)} %get-tuple-element.2) | data formatting | bytes 393216
  31.6 0.6 %copy.11 = f32[2,6,8,128]{3,2,1,0:T(8,128)} copy(f32[2,6,8,128]{3,2,1,0:T(8,128)S(1)} %get-tuple-element.3) | data formatting | bytes 98304

commit v5 on v4

--- a/solution.py
+++ b/solution.py
@@ -124,8 +124,8 @@
             pl.semaphore_signal(barrier, inc=1, device_id=peer(off), device_id_type=MESH)
 
 
-    pairs_in = (
-        (vel_in, vel), (conv_w_in, conv_w), (lift_w_in, lift_w), (lift_b_in, lift_b),
+    pairs_in = tuple((vel_in.at[n], vel.at[n]) for n in range(4)) + (
+        (conv_w_in, conv_w), (lift_w_in, lift_w), (lift_b_in, lift_b),
         (conv_b_in, conv_b), (head_w_in, head_w),
     )
     loads = [
@@ -162,8 +162,9 @@
     picker = jnp.where((iota((16, 256), 1) // 2 == ends) & (r16 < 8), 1.0, 0.0).astype(BF16)
     csend[...] = jnp.zeros_like(csend)
     ystage[...] = jnp.zeros_like(ystage)
-    loads[0].wait()
-    for p in range(2):
+    for p in range(2):
+        loads[2 * p].wait()
+        loads[2 * p + 1].wait()
         for c in range(3):
             both = vel[2 * p, c] + vel[2 * p + 1, c]
             r = 16 * (3 * p + c)
@@ -197,12 +198,6 @@
             for n in range(1, 4):
                 row = row + spaced[4 * t + n : 4 * t + n + 1]
             cpack[t, p] = row
-    cwide[...] = jnp.zeros_like(cwide)
-    for k in range(12):
-        yvstage[0, 4 * k : 4 * k + 4, :] = vel[k // 3, k % 3, 12:16, :]
-        yvstage[1, 4 * k : 4 * k + 4, :] = vel[k // 3, k % 3, 0:4, :]
-    for s in range(2):
-        yvsend[s] = packed(yvstage[s], s)
 
     pl.semaphore_wait(
         barrier, len(NEAR) - jnp.where(leftmost, len(BEYOND), 0) + len(FAR) * odd
@@ -251,7 +246,14 @@
 
     xbox = [send(bx.at[1], xland.at[0], (0, 0, -1)), send(bx.at[0], xland.at[1], (0, 0, 1))]
 
-    for load in loads[1:]:
+    for k in range(12):
+        yvstage[0, 4 * k : 4 * k + 4, :] = vel[k // 3, k % 3, 12:16, :]
+        yvstage[1, 4 * k : 4 * k + 4, :] = vel[k // 3, k % 3, 0:4, :]
+    for s in range(2):
+        yvsend[s] = packed(yvstage[s], s)
+    cwide[...] = jnp.zeros_like(cwide)
+
+    for load in loads[4:]:
         load.wait()
     for k in range(9):
         a, c = k // 3, k % 3
@@ -576,7 +578,7 @@
         pltpu.VMEM((2, 3, 2, 16, 128), F32),
         pltpu.SemaphoreType.DMA((ncopies,)),
         pltpu.SemaphoreType.DMA((ncopies,)),
-        pltpu.SemaphoreType.DMA((6,)),
+        pltpu.SemaphoreType.DMA((9,)),
         pltpu.SemaphoreType.REGULAR,
         pltpu.SemaphoreType.REGULAR,
     ]

time: 32.4 us -> 32.5 us (level)
  no operation moved by 1% of the time
where the time goes in v5:
time: 32.5 us; the launch traced here: 32.3 us
  Pallas kernels  30.3 us (93%)
  local copies, waits for them, and re-layouts  1.3 us (4%)
  between operations  0.64 us (2%)
    pallas_call x1, Pallas kernels, body(): pl.pallas_call(body_kernel, out_shape=(pltpu.VMEM((4, 3, 16, 256), F32),...  30.3 us
    unnamed x2, local copies, waits for them, and re-layouts  1.3 us

profile of v5, /device:TPU:1, one launch (start us, length us, event | category | flops | bytes accessed | tf_op | source)
XLA Modules:
  0.0 32.3 jit_solution(9553879324062935852)
XLA Ops:
  0.6 30.3 %shard_map.77 = (f32[4,3,16,256]{3,2,1,0:T(8,128)S(1)}, f32[2,6,8,128]{3,2,1,0:T(8,128)S(1)}) custom-call(f32[4,3,16,256]{3,2,1,0:T(8,128)} %vel_in.1, f32[3,32]{1,0:T(4,128)} %bitcast.3, f32[1,32]{1,0:T(1,128)} %bitcast.4, bf16[27,8,32]{2,1,0:T(8,128)(2,1)} %conv_w_in.1, bf16[1,8]{1,0:T(2,128)(2,1)} %bitcast.5, bf16[6,8]{1,0:T(8,128)(2,1)} %head_w_in.1), custom_call_target="tpu_custom_call" | custom-call | tf_op jit(solution)/shard_map/pallas_call | solution.py:585
  31.0 0.7 %copy.10 = f32[4,3,16,256]{3,2,1,0:T(8,128)} copy(f32[4,3,16,256]{3,2,1,0:T(8,128)S(1)} %get-tuple-element.2) | data formatting | bytes 393216
  31.6 0.6 %copy.11 = f32[2,6,8,128]{3,2,1,0:T(8,128)} copy(f32[2,6,8,128]{3,2,1,0:T(8,128)S(1)} %get-tuple-element.3) | data formatting | bytes 98304
